TPU v7x, 256 devices: a whole 4x4x8 slice. The times are simulated.
256 devices in a mesh: expert: 16 (over x_lo, z), tensor: 8 (over y, x_hi), pair: 2 (over core).
Axes of the slice: x: 4 (x_hi: 2, x_lo: 2; x = x_hi * 2 + x_lo), y: 4, z: 8, core: 2. Of those that a mesh axis runs over, the one named last changes fastest.
Arguments:
- context: bfloat16 [2048, 4096], P('expert', 'tensor'), may hold values from -6 to 6
- out_weight: bfloat16 [4096, 4096], P('tensor', 'pair'), may hold values from -0.09375 to 0.09375
- residual: bfloat16 [2048, 4096], P(('expert', 'tensor'), 'pair'), may hold values from -6 to 6
- norm_gain: bfloat16 [4096], replicated, may hold values from 0.099609375 to 1.8984375
- expert_ids: int32 [2048, 8], P(('expert', 'tensor')), may hold values from 0 to 127, all different within a row; in each aligned block of 16 rows (0 to 15, 16 to 31, ...) at most 2 rows name the same one
- route_prob: float32 [2048, 8], P(('expert', 'tensor')), may hold values from 0.02 to 1
- w_gate: bfloat16 [128, 4096, 768], P(('expert', 'tensor'), None, 'pair'), may hold values from -0.09375 to 0.09375
- w_up: bfloat16 [128, 4096, 768], P(('expert', 'tensor'), None, 'pair'), may hold values from -0.09375 to 0.09375
- w_down: bfloat16 [128, 768, 4096], P(('expert', 'tensor'), 'pair'), may hold values from -0.21875 to 0.21875
Outputs:
- layer_out: bfloat16 [2048, 4096], P(('expert', 'tensor'), 'pair')
Inputs may be any that keep to these rules, and one draw needn't show every extreme that they name: `expert_ids`: each row names 8 different experts. In each aligned block of 16 rows (the rows of one device) no expert is named by more than 2 rows, a bound that some block reaches.
All inputs are finite; a program needn't handle non-finite values.
Results may differ from a plain program's by a relative error of at most 0.0052.
Values may be sent and summed in bfloat16 or wider, within the bound.
A program may use at most 64 MiB of HBM per device.

v0:
```python
import jax
import jax.numpy as jnp
from jax import lax
from jax.sharding import PartitionSpec as P

EPS = 1e-06


def expert_mlp(arrived, w_gate, w_up, w_down, group_count):
    item_count = arrived.shape[0]
    local_experts = w_gate.shape[0]
    layer_inputs = arrived.reshape(item_count, group_count, local_experts, arrived.shape[2])
    gate_values = jnp.einsum(
        "ksed,edf->ksef", layer_inputs, w_gate, preferred_element_type=jnp.float32
    )
    up_values = jnp.einsum("ksed,edf->ksef", layer_inputs, w_up, preferred_element_type=jnp.float32)
    hidden = (jax.nn.silu(gate_values) * up_values).astype(jnp.bfloat16)
    return jnp.einsum("ksef,efd->ksed", hidden, w_down, preferred_element_type=jnp.float32)


def body(context, out_weight, residual, norm_gain, expert_ids, route_prob, w_gate, w_up, w_down):
    group_count = lax.axis_size(("expert", "tensor"))
    token_rows = residual.shape[0]
    half_width = residual.shape[1]
    top_count = expert_ids.shape[1]
    local_experts = w_gate.shape[0]
    expert_count = local_experts * group_count
    capacity = max(2, (5 * token_rows * top_count + 4 * expert_count - 1) // (4 * expert_count))
    attention_output = lax.psum_scatter(
        jnp.dot(context, out_weight, preferred_element_type=jnp.float32),
        "tensor",
        scatter_dimension=0,
        tiled=True,
    )
    stream = (residual.astype(jnp.float32) + attention_output).astype(jnp.bfloat16)
    full_rows = lax.all_gather(stream, "pair", axis=1, tiled=True).astype(jnp.float32)
    norm_scale = lax.rsqrt(jnp.mean(full_rows * full_rows, axis=1, keepdims=True) + EPS)
    normed = (full_rows * norm_scale * norm_gain.astype(jnp.float32)).astype(jnp.bfloat16)
    flat_ids = expert_ids.reshape(token_rows * top_count)
    expert_marks = (flat_ids[:, None] == jnp.arange(expert_count, dtype=jnp.int32)[None, :]).astype(
        jnp.int32
    )
    slot_index = jnp.sum((jnp.cumsum(expert_marks, axis=0) - expert_marks) * expert_marks, axis=1)
    target_slot = slot_index * expert_count + flat_ids
    slot_columns = jnp.arange(capacity * expert_count, dtype=jnp.int32)
    place_table = (target_slot[:, None] == slot_columns[None, :]).astype(jnp.bfloat16)
    token_table = jnp.sum(
        place_table.reshape(token_rows, top_count, capacity * expert_count), axis=1
    )
    outgoing = jnp.einsum("rs,rd->sd", token_table, normed, preferred_element_type=jnp.float32)
    outgoing = outgoing.astype(jnp.bfloat16).reshape(capacity, expert_count, normed.shape[1])
    partial_out = expert_mlp(
        lax.all_to_all(outgoing, ("expert", "tensor"), split_axis=1, concat_axis=1, tiled=True),
        w_gate,
        w_up,
        w_down,
        group_count,
    )
    item_count = partial_out.shape[0]
    summed = lax.psum_scatter(
        partial_out.astype(jnp.bfloat16), "pair", scatter_dimension=3, tiled=True
    )
    summed = summed.reshape(item_count, expert_count, half_width)
    returned_tokens = lax.all_to_all(
        summed, ("expert", "tensor"), split_axis=1, concat_axis=1, tiled=True
    )
    flat_returned = returned_tokens.reshape(capacity * expert_count, returned_tokens.shape[2])
    picked = jnp.dot(place_table, flat_returned, preferred_element_type=jnp.float32)
    picked = picked.reshape(token_rows, top_count, returned_tokens.shape[2])
    weights = route_prob / jnp.sum(route_prob, axis=1, keepdims=True)
    mixture = jnp.sum(weights[:, :, None] * picked, axis=1)
    return (stream.astype(jnp.float32) + mixture).astype(jnp.bfloat16)


def solution(mesh):
    placed = (
        P("expert", "tensor"),
        P("tensor", "pair"),
        P(("expert", "tensor"), "pair"),
        P(),
        P(("expert", "tensor"), None),
        P(("expert", "tensor"), None),
        P(("expert", "tensor"), None, "pair"),
        P(("expert", "tensor"), None, "pair"),
        P(("expert", "tensor"), "pair", None),
    )
    return jax.shard_map(
        body, mesh=mesh, in_specs=placed, out_specs=P(("expert", "tensor"), "pair"), check_vma=False
    )
```

profile of v0, /device:TPU:8, one launch (start us, length us, event | category | flops | bytes accessed | tf_op | source)
XLA Modules:
  0.0 241.6 jit_solution(11503350973342128017)
XLA Ops:
  6.5 0.0 reduce-scatter.3.cloned.1.call-start
  6.6 3.2 %fusion.57 = f32[128,2048]{1,0:T(8,128)} fusion(bf16[128,512]{1,0:T(8,128)(2,1)} %param.9, bf16[512,2048]{1,0:T(8,128)(2,1)} %param.10), kind=kOutput, calls=%fused_computation.45 | convolution fusion | flops 268435456 | bytes 3276800 | tf_op jit(solution)/shard_map/dot_general | solution.py:30
  9.8 0.0 reduce-scatter.3.cloned.1.call-update
  9.9 0.0 reduce-scatter.5.cloned.1.call-start
  9.9 0.0 copy-done.5
  9.9 0.1 copy.25
  10.0 0.1 eq.51
  10.1 0.1 fusion.55
  10.2 0.2 reduce_window_sum.11
  10.3 0.2 select_reduce_fusion
  10.5 0.1 mul.54
  10.6 0.1 fusion.53
  10.8 79.8 %reduce-scatter.3.cloned.1.call-done = f32[16,2048]{1,0:T(8,128)} async-done(((f32[128,2048]{1,0:T(8,128)}), f32[16,2048]{1,0:T(8,128)}) %reduce-scatter.3.cloned.1.call-update) | async-done | bytes 131088 | tf_op jit(solution)/shard_map/reduce_scatter | solution.py:29
  90.6 0.9 add_convert_fusion.1
  91.5 1.9 all_gather.3
  93.4 0.1 fusion.43
  93.5 0.8 convolution_convert_fusion.1
  94.3 2.2 copy.27
  96.5 0.0 copy-start.6
  96.5 65.2 %all_to_all.10 = bf16[2,128,4096]{2,0,1:T(2,128)(2,1)S(1)} all-to-all(bf16[2,128,4096]{2,0,1:T(2,128)(2,1)S(1)} %copy.27), channel_id=1, replica_groups=mesh['expert'=16,'tensor'=8,'pair'=2] {'expert','tensor'}, dimensions={1} | all-to-all | bytes 4194304 | tf_op jit(solution)/shard_map/all_to_all | solution.py:53
  161.7 1.3 copy-done.1
  163.0 3.5 %fusion.9 = f32[2,128,1,384]{3,1,0,2:T(8,128)} fusion(bf16[1,4096,384]{2,1,0:T(8,128)(2,1)S(1)} %copy-done.6, bf16[2,128,4096]{2,0,1:T(2,128)(2,1)S(1)} %all_to_all.10), kind=kOutput, calls=%fused_computation.12 | convolution fusion | flops 805306368 | bytes 5636096 | tf_op jit(solution)/shard_map/ksed,edf->ksef/dot_general | solution.py:13
  166.6 7.8 %fusion = bf16[2,128,1,4096]{3,1,0,2:T(8,128)(2,1)} fusion(bf16[1,384,4096]{2,1,0:T(8,128)(2,1)S(1)} %copy-done, bf16[1,4096,384]{2,1,0:T(8,128)(2,1)} %param.16, bf16[2,128,4096]{2,0,1:T(2,128)(2,1)} %copy-done.1, f32[2,128,1,384]{3,1,0,2:T(8,128)} %fusion.9), kind=kOutput, calls=%fused_computation.2 | convolution fusion | flops 1612251136 | bytes 10878976 | tf_op jit(solution)/shard_map/ksef,efd->ksed/dot_general | solution.py:18
  174.4 0.0 reduce-scatter.5.cloned.1.call-update
  174.4 9.4 %reduce-scatter.5.cloned.1.call-done = bf16[2,128,1,2048]{3,1,0,2:T(8,128)(2,1)} async-done(((bf16[2,128,1,4096]{3,1,0,2:T(8,128)(2,1)}), bf16[2,128,1,2048]{3,1,0,2:T(8,128)(2,1)}) %reduce-scatter.5.cloned.1.call-update) | async-done | bytes 1048592 | tf_op jit(solution)/shard_map/reduce_scatter | solution.py:60
  183.8 3.3 %copy.30 = bf16[2,128,2048]{2,0,1:T(2,128)(2,1)} copy(bf16[2,128,2048]{2,1,0:T(8,128)(2,1)} %bitcast.67) | data formatting | bytes 2097152 | tf_op jit(solution)/shard_map/reshape | solution.py:63
  187.1 14.2 %all-to-all-start.1 = ((bf16[2,128,2048]{2,0,1:T(2,128)(2,1)}), bf16[2,128,2048]{2,0,1:T(2,128)(2,1)}, u32[]{:S(2)}, u32[]{:S(2)}) async-start(bf16[2,128,2048]{2,0,1:T(2,128)(2,1)} %copy.30), calls=%async_computation.3 | async-start | bytes 2097152 | tf_op jit(solution)/shard_map/all_to_all | solution.py:64
  201.4 0.1 copy.24
  201.5 30.6 %all-to-all-done.1 = bf16[2,128,2048]{2,0,1:T(2,128)(2,1)} async-done(((bf16[2,128,2048]{2,0,1:T(2,128)(2,1)}), bf16[2,128,2048]{2,0,1:T(2,128)(2,1)}, u32[]{:S(2)}, u32[]{:S(2)}) %all-to-all-start.1) | async-done | bytes 1048608 | tf_op jit(solution)/shard_map/all_to_all | solution.py:64
  232.0 1.6 copy.31
  233.6 0.5 fusion.8
  234.1 0.6 add_convert_fusion
  (17 shorter events, 0.1 us)
Async XLA Ops:
  6.5 160.0 %copy-start = (bf16[1,384,4096]{2,1,0:T(8,128)(2,1)S(1)}, bf16[1,384,4096]{2,1,0:T(8,128)(2,1)}, u32[]{:S(2)}) copy-start(bf16[1,384,4096]{2,1,0:T(8,128)(2,1)} %param.17) | copy-start | bytes 9437188
  6.5 3.4 %copy-start.5 = (s32[16,8]{0,1:T(8,128)S(1)}, s32[16,8]{0,1:T(8,128)}, u32[]{:S(2)}) copy-start(s32[16,8]{0,1:T(8,128)} %param.13) | copy-start | bytes 1540
  6.5 4.1 %copy-start.4 = (bf16[4096]{0:T(1024)(128)(2,1)S(1)}, bf16[4096]{0:T(1024)(128)(2,1)}, u32[]{:S(2)}) copy-start(bf16[4096]{0:T(1024)(128)(2,1)} %param.12) | copy-start | bytes 24580
  6.5 84.0 %copy-start.2 = (bf16[16,2048]{1,0:T(8,128)(2,1)S(1)}, bf16[16,2048]{1,0:T(8,128)(2,1)}, u32[]{:S(2)}) copy-start(bf16[16,2048]{1,0:T(8,128)(2,1)} %param.11) | copy-start | bytes 196612
  6.5 84.0 %reduce-scatter.3.cloned.1.call-start = ((), (), s32[]{:S(2)}) async-start(), calls=%async_computation.4 | async-start | bytes 1179648 | tf_op jit(solution)/shard_map/reduce_scatter | solution.py:29
  9.9 174.0 %reduce-scatter.5.cloned.1.call-start = ((), (), s32[]{:S(2)}) async-start(), calls=%async_computation.5 | async-start | bytes 3145728 | tf_op jit(solution)/shard_map/reduce_scatter | solution.py:60
  96.5 66.5 %copy-start.6 = (bf16[1,4096,384]{2,1,0:T(8,128)(2,1)S(1)}, bf16[1,4096,384]{2,1,0:T(8,128)(2,1)}, u32[]{:S(2)}) copy-start(bf16[1,4096,384]{2,1,0:T(8,128)(2,1)} %param.15) | copy-start | bytes 9437188
  161.7 1.3 copy-start.1
  183.8 17.5 %copy-start.3 = (f32[16,8]{0,1:T(8,128)S(1)}, f32[16,8]{0,1:T(8,128)}, u32[]{:S(2)}) copy-start(f32[16,8]{0,1:T(8,128)} %param.14) | copy-start | bytes 1540
  187.1 44.9 %all-to-all-start.1 = ((bf16[2,128,2048]{2,0,1:T(2,128)(2,1)}), bf16[2,128,2048]{2,0,1:T(2,128)(2,1)}, u32[]{:S(2)}, u32[]{:S(2)}) async-start(bf16[2,128,2048]{2,0,1:T(2,128)(2,1)} %copy.30), calls=%async_computation.3 | async-start | bytes 2097152 | tf_op jit(solution)/shard_map/all_to_all | solution.py:64
Sparse Core Ops, SparseCore 0:
  11.2 79.2 reduce-scatter.2
  174.5 9.2 reduce-scatter.4
where the time goes:
time: 242 us
  waiting for transfers between devices  120 us (50%)
  blocking collectives  67.1 us (28%)
  matrix products  15.8 us (7%)
  starting transfers between devices  14.3 us (6%)
  between operations  13.5 us (6%)
  local copies, waits for them, and re-layouts  8.7 us (4%)
    reduce_scatter x1, waiting for transfers between devices, body(): lax.psum_scatter(jnp.dot(context, out_weight, preferred_element_type=jnp....  79.8 us
    all_to_all x1, blocking collectives, body(): lax.all_to_all(outgoing, ('expert', 'tensor'), split_axis=1, concat_axis=...  65.2 us
    all_to_all x1, waiting for transfers between devices, body(): lax.all_to_all(summed, ('expert', 'tensor'), split_axis=1, concat_axis=1,...  30.6 us
    all_to_all x1, starting transfers between devices, body(): lax.all_to_all(summed, ('expert', 'tensor'), split_axis=1, concat_axis=1,...  14.2 us
    reduce_scatter x1, waiting for transfers between devices, body(): lax.psum_scatter(partial_out.astype(jnp.bfloat16), 'pair', scatter_dimens...  9.4 us
    dot_general x1, matrix products, expert_mlp(): jnp.einsum('ksef,efd->ksed', hidden, w_down, preferred_element_type=jnp.f...  7.83 us
  transfers between devices with their start and end apart: 3, of which 3 were waited for; matrix products, arithmetic and copies ran while one was open for 0% of the time, Pallas kernels for 0%

commit v1 on v0

v1 whole, which is shorter than its diff:
```python
import functools

import jax
import jax.numpy as jnp
from jax import lax
from jax.experimental import pallas as pl
from jax.experimental.pallas import tpu as pltpu
from jax.sharding import PartitionSpec as P

EPS = 1e-06
MESH = pl.DeviceIdType.MESH
BF16 = jnp.bfloat16
F32 = jnp.float32
ROWS = 16
NZ = 8
NT = 8
NQ = 16
CHUNKS = 4


def dot(a, b):
    return jnp.dot(a, b, preferred_element_type=F32)


def dot_nt(a, b):
    return lax.dot_general(a, b, (((1,), (1,)), ((), ())), preferred_element_type=F32)


def rows16(index):
    return pl.ds(pl.multiple_of(index * ROWS, ROWS), ROWS)


def kernel(
    ctx_hbm, ow_hbm, res_hbm, gain_hbm, ids_hbm, prob_hbm, wg_hbm, wu_hbm, wd_hbm, out_ref,
    ctx, ow, res, gain, ids, prob, wgu, wd,
    attb, ars, stream, ssq, meta, metal, table, chi, clo,
    line, disp, xs, acc, hid, outb, ret, mixb, zr,
    ld, ow_sem, w_sem,
    a_send, a_recv, m_sem, wd_sem, s_sem, g_send, g_recv, d_send, d_recv, f_send, f_recv,
    h_sem, r_send, r_recv, z_send, z_recv,
):
    e, t, p = lax.axis_index("expert"), lax.axis_index("tensor"), lax.axis_index("pair")
    z, x_lo = lax.rem(e, NZ), lax.div(e, NZ)
    y, x_hi = lax.div(t, 2), lax.rem(t, 2)
    x = x_hi * 2 + x_lo
    q = x_lo * NT + t
    half = ow.shape[2] * CHUNKS
    width = half // CHUNKS
    ff = wg_hbm.shape[2]
    partner = (e, t, 1 - p)

    def z_peer(j):
        return (x_lo * NZ + lax.rem(z + j, NZ), t, p)

    def plane_peer(j):
        px, py = lax.rem(x + lax.rem(j, 4), 4), lax.rem(y + lax.div(j, 4), 4)
        plo, pt = lax.rem(px, 2), py * 2 + lax.div(px, 2)
        return plo * NT + pt, (plo * NZ + z, pt, p)

    def each(count, fn):
        def step(j, carry):
            fn(j)
            return carry
        lax.fori_loop(1, count, step, 0)

    def remote(src, dst, send, recv, device):
        return pltpu.make_async_remote_copy(
            src_ref=src, dst_ref=dst, send_sem=send, recv_sem=recv,
            device_id=device, device_id_type=MESH,
        )

    def wait_bytes(ref, sem):
        pltpu.make_async_copy(ref, ref, sem).wait()

    barrier = pltpu.get_barrier_semaphore()
    pl.semaphore_signal(barrier, inc=1, device_id=partner, device_id_type=MESH)
    each(NZ, lambda j: pl.semaphore_signal(barrier, inc=1, device_id=z_peer(j), device_id_type=MESH))
    each(NQ, lambda j: pl.semaphore_signal(barrier, inc=1, device_id=plane_peer(j)[1], device_id_type=MESH))

    def mine(index):
        return pl.ds(pl.multiple_of(index * half, half), half)

    loads = [
        pltpu.make_async_copy(ids_hbm, ids, ld.at[0]),
        pltpu.make_async_copy(prob_hbm, prob, ld.at[1]),
        pltpu.make_async_copy(ctx_hbm, ctx, ld.at[2]),
        pltpu.make_async_copy(res_hbm, res, ld.at[3]),
        pltpu.make_async_copy(gain_hbm.at[:, mine(p)], gain, ld.at[4]),
    ]
    ow_loads = [
        pltpu.make_async_copy(ow_hbm.at[:, pl.ds(c * width, width)], ow.at[c], ow_sem.at[c])
        for c in range(CHUNKS)
    ]
    w_loads = []
    for k, side in enumerate((p, 1 - p)):
        w_loads.append(pltpu.make_async_copy(
            wg_hbm.at[0, mine(side), :], wgu.at[k, :, pl.ds(0, ff)], w_sem.at[2 * k]))
        w_loads.append(pltpu.make_async_copy(
            wu_hbm.at[0, mine(side), :], wgu.at[k, :, pl.ds(ff, ff)], w_sem.at[2 * k + 1]))
    wd_load = pltpu.make_async_copy(wd_hbm.at[0, :, mine(p)], wd.at[0], w_sem.at[4])
    for copy in loads[:3] + ow_loads + loads[3:] + w_loads + [wd_load]:
        copy.start()

    loads[0].wait()
    loads[1].wait()
    weights = prob[...] / jnp.sum(prob[...], axis=1, keepdims=True)
    named = ids[...]
    lanes = lax.broadcasted_iota(jnp.int32, (ROWS, 128), 1)
    mark = jnp.zeros((ROWS, 128), F32)
    spread = jnp.zeros((ROWS, 128), F32)
    for k in range(named.shape[1]):
        same = lanes == named[:, k:k + 1]
        mark = jnp.where(same, 1.0, mark)
        spread = jnp.where(same, weights[:, k:k + 1], spread)
    earlier = (
        lax.broadcasted_iota(jnp.int32, (ROWS, ROWS), 1)
        < lax.broadcasted_iota(jnp.int32, (ROWS, ROWS), 0)
    ).astype(F32).astype(BF16)
    code = mark * (1.0 + dot(earlier, mark.astype(BF16)))
    high = spread.astype(BF16)
    meta[0] = code.astype(BF16)
    meta[1] = high
    meta[2] = (spread - high.astype(F32)).astype(BF16)
    metal[:, rows16(z), :] = meta[...]

    loads[2].wait()

    def project(c):
        ow_loads[c].wait()
        attb[c] = dot(ctx[...], ow[c]).astype(BF16)

    def scatter_heads(c):
        def send(j):
            pt = lax.rem(t + j, NT)
            remote(attb.at[c, rows16(pt), :], ars.at[c, rows16(t), :],
                   a_send.at[c], a_recv.at[c], (e, pt, p)).start()
        each(NT, send)

    project(0)
    pl.semaphore_wait(barrier, NZ - 1 + NQ - 1 + 1)
    scatter_heads(0)
    each(NZ, lambda j: remote(meta, metal.at[:, rows16(z), :], m_sem.at[0], m_sem.at[1], z_peer(j)).start())
    for c in range(1, CHUNKS):
        project(c)
        scatter_heads(c)
    wd_swap = remote(wd_hbm.at[0, :, mine(1 - p)], wd.at[1], wd_sem.at[0], wd_sem.at[1], partner)
    wd_swap.start()

    wait_bytes(metal.at[:, pl.ds(0, (NZ - 1) * ROWS), :], m_sem.at[1])
    slots = NQ * ROWS
    tokens = NZ * ROWS

    def expert_of(row):
        place = lax.shift_right_logical(row, 4)
        return (lax.shift_right_logical(place, 3) * (NZ * NT) + z * NT + (place & (NT - 1)))

    pick = (
        lax.broadcasted_iota(jnp.int32, (slots, 128), 1)
        == expert_of(lax.broadcasted_iota(jnp.int32, (slots, 128), 0))
    ).astype(F32).astype(BF16)

    def fits(row, token, codes):
        wanted = ((row & 1) + 1).astype(F32)
        same = (lax.shift_right_logical(row, 1) & (NZ - 1)) == lax.shift_right_logical(token, 4)
        return same & (codes == wanted)

    down_rows = lax.broadcasted_iota(jnp.int32, (slots, tokens), 0)
    down_toks = lax.broadcasted_iota(jnp.int32, (slots, tokens), 1)
    table[...] = jnp.where(fits(down_rows, down_toks, dot_nt(pick, metal[0])), 1.0, 0.0).astype(BF16)
    up_rows = lax.broadcasted_iota(jnp.int32, (tokens, slots), 1)
    up_toks = lax.broadcasted_iota(jnp.int32, (tokens, slots), 0)
    chosen = fits(up_rows, up_toks, dot_nt(metal[0], pick))
    chi[...] = jnp.where(chosen, dot_nt(metal[1], pick), 0.0).astype(BF16)
    clo[...] = jnp.where(chosen, dot_nt(metal[2], pick), 0.0).astype(BF16)

    loads[3].wait()
    loads[4].wait()
    squares = jnp.zeros((ROWS, 1), F32)
    for c in range(CHUNKS):
        ars[c, rows16(t), :] = attb[c, rows16(t), :]
        wait_bytes(ars.at[c, pl.ds(0, (NT - 1) * ROWS), :], a_recv.at[c])
        total = ars[c, 0:ROWS, :].astype(F32)
        for k in range(1, NT):
            total += ars[c, k * ROWS:(k + 1) * ROWS, :].astype(F32)
        part = (res[:, c * width:(c + 1) * width].astype(F32) + total).astype(BF16)
        stream[c] = part
        wide = part.astype(F32)
        squares += jnp.sum(wide * wide, axis=1, keepdims=True)
    ssq[0] = jnp.broadcast_to(squares, (ROWS, 128))
    swap = remote(ssq.at[0], ssq.at[1], s_sem.at[0], s_sem.at[1], partner)
    swap.start()
    swap.wait()
    mean = (ssq[0] + ssq[1])[:, 0:1] * (1.0 / (2 * half))
    scale = lax.rsqrt(mean + EPS)
    for c in range(CHUNKS):
        rows = stream[c].astype(F32) * scale * gain[:, c * width:(c + 1) * width].astype(F32)
        line[c, rows16(z), :] = rows.astype(BF16)
        each(NZ, lambda j: remote(line.at[c, rows16(z), :], line.at[c, rows16(z), :],
                                  g_send.at[c], g_recv.at[c], z_peer(j)).start())

    for copy in w_loads:
        copy.wait()

    def dispatch(c):
        wait_bytes(line.at[c, pl.ds(0, tokens - ROWS), :], g_recv.at[c])
        disp[c] = dot(table[...], line[c]).astype(BF16)

        def send(j):
            pq, device = plane_peer(j)
            remote(disp.at[c, rows16(pq), :], xs.at[0, c, rows16(q), :],
                   d_send.at[c], d_recv.at[c], device).start()
        each(NQ, send)
        xs[0, c, rows16(q), :] = disp[c, rows16(q), :]

    forwards = [
        remote(xs.at[0, c], xs.at[1, c], f_send.at[c], f_recv.at[c], partner) for c in range(CHUNKS)
    ]

    def forward(c):
        wait_bytes(xs.at[0, c, pl.ds(0, slots - ROWS), :], d_recv.at[c])
        forwards[c].start()

    def multiply(c):
        cols = pl.ds(c * width, width)
        own = dot(xs[0, c], wgu[0, cols, :])
        forwards[c].wait_recv()
        both = own + dot(xs[1, c], wgu[1, cols, :])
        if c == 0:
            acc[...] = both
        else:
            acc[...] += both

    for c in range(CHUNKS + 2):
        if c < CHUNKS:
            dispatch(c)
        if 1 <= c <= CHUNKS:
            forward(c - 1)
        if c >= 2:
            multiply(c - 2)

    gate, up = acc[:, 0:ff], acc[:, ff:2 * ff]
    hid[0] = (gate / (1.0 + jnp.exp(-gate)) * up).astype(BF16)
    hid_swap = remote(hid.at[0], hid.at[1], h_sem.at[0], h_sem.at[1], partner)
    hid_swap.start()
    wd_load.wait()
    wd_swap.wait_recv()
    hid_swap.wait_recv()

    def produce(c):
        cols = pl.ds(c * width, width)
        outb[c] = (dot(hid[0], wd[0, :, cols]) + dot(hid[1], wd[1, :, cols])).astype(BF16)

        def send(j):
            pq, device = plane_peer(j)
            remote(outb.at[c, rows16(pq), :], ret.at[c, rows16(q), :],
                   r_send.at[c], r_recv.at[c], device).start()
        each(NQ, send)
        ret[c, rows16(q), :] = outb[c, rows16(q), :]

    def mix(c):
        wait_bytes(ret.at[c, pl.ds(0, slots - ROWS), :], r_recv.at[c])
        mixb[c] = (dot(chi[...], ret[c]) + dot(clo[...], ret[c])).astype(BF16)

        def send(j):
            there = lax.rem(z + j, NZ)
            remote(mixb.at[c, rows16(there), :], zr.at[c, rows16(z), :],
                   z_send.at[c], z_recv.at[c], z_peer(j)).start()
        each(NZ, send)
        zr[c, rows16(z), :] = mixb[c, rows16(z), :]

    def finish(c):
        wait_bytes(zr.at[c, pl.ds(0, tokens - ROWS), :], z_recv.at[c])
        total = stream[c].astype(F32)
        for k in range(NZ):
            total += zr[c, k * ROWS:(k + 1) * ROWS, :].astype(F32)
        out_ref[:, c * width:(c + 1) * width] = total.astype(BF16)

    for c in range(CHUNKS):
        produce(c)
    for c in range(CHUNKS + 1):
        if c < CHUNKS:
            mix(c)
        if c >= 1:
            finish(c - 1)

    wait_bytes(metal.at[:, pl.ds(0, (NZ - 1) * ROWS), :], m_sem.at[0])
    wd_swap.wait_send()
    hid_swap.wait_send()
    for c in range(CHUNKS):
        wait_bytes(ars.at[c, pl.ds(0, (NT - 1) * ROWS), :], a_send.at[c])
        wait_bytes(line.at[c, pl.ds(0, tokens - ROWS), :], g_send.at[c])
        wait_bytes(xs.at[0, c, pl.ds(0, slots - ROWS), :], d_send.at[c])
        forwards[c].wait_send()
        wait_bytes(ret.at[c, pl.ds(0, slots - ROWS), :], r_send.at[c])
        wait_bytes(zr.at[c, pl.ds(0, tokens - ROWS), :], z_send.at[c])


def body(context, out_weight, residual, norm_gain, expert_ids, route_prob, w_gate, w_up, w_down):
    rows, half = residual.shape
    group, depth = context.shape
    ff = w_gate.shape[2]
    width = half // CHUNKS
    slots, tokens = NQ * ROWS, NZ * ROWS
    dma = pltpu.SemaphoreType.DMA
    scratch = [
        pltpu.VMEM((group, depth), BF16),
        pltpu.VMEM((CHUNKS, depth, width), BF16),
        pltpu.VMEM((rows, half), BF16),
        pltpu.VMEM((1, half), BF16),
        pltpu.VMEM(expert_ids.shape, jnp.int32),
        pltpu.VMEM(route_prob.shape, F32),
        pltpu.VMEM((2, half, 2 * ff), BF16),
        pltpu.VMEM((2, ff, half), BF16),
        pltpu.VMEM((CHUNKS, group, width), BF16),
        pltpu.VMEM((CHUNKS, group, width), BF16),
        pltpu.VMEM((CHUNKS, rows, width), BF16),
        pltpu.VMEM((2, rows, 128), F32),
        pltpu.VMEM((3, rows, 128), BF16),
        pltpu.VMEM((3, tokens, 128), BF16),
        pltpu.VMEM((slots, tokens), BF16),
        pltpu.VMEM((tokens, slots), BF16),
        pltpu.VMEM((tokens, slots), BF16),
        pltpu.VMEM((CHUNKS, tokens, width), BF16),
        pltpu.VMEM((CHUNKS, slots, width), BF16),
        pltpu.VMEM((2, CHUNKS, slots, width), BF16),
        pltpu.VMEM((slots, 2 * ff), F32),
        pltpu.VMEM((2, slots, ff), BF16),
        pltpu.VMEM((CHUNKS, slots, width), BF16),
        pltpu.VMEM((CHUNKS, slots, width), BF16),
        pltpu.VMEM((CHUNKS, tokens, width), BF16),
        pltpu.VMEM((CHUNKS, tokens, width), BF16),
        dma((5,)), dma((CHUNKS,)), dma((5,)),
        dma((CHUNKS,)), dma((CHUNKS,)), dma((2,)), dma((2,)), dma((2,)),
        dma((CHUNKS,)), dma((CHUNKS,)), dma((CHUNKS,)), dma((CHUNKS,)),
        dma((CHUNKS,)), dma((CHUNKS,)),
        dma((2,)), dma((CHUNKS,)), dma((CHUNKS,)), dma((CHUNKS,)), dma((CHUNKS,)),
    ]
    return pl.pallas_call(
        kernel,
        out_shape=jax.ShapeDtypeStruct((rows, half), BF16),
        in_specs=[pl.BlockSpec(memory_space=pl.ANY)] * 9,
        out_specs=pl.BlockSpec(memory_space=pltpu.VMEM),
        scratch_shapes=scratch,
        compiler_params=pltpu.CompilerParams(
            collective_id=0, has_side_effects=True, vmem_limit_bytes=48 * 1024 * 1024
        ),
        name="block",
    )(
        context, out_weight, residual, norm_gain.reshape(1, -1), expert_ids, route_prob,
        w_gate, w_up, w_down,
    )


def solution(mesh):
    placed = (
        P("expert", "tensor"),
        P("tensor", "pair"),
        P(("expert", "tensor"), "pair"),
        P(),
        P(("expert", "tensor"), None),
        P(("expert", "tensor"), None),
        P(("expert", "tensor"), None, "pair"),
        P(("expert", "tensor"), None, "pair"),
        P(("expert", "tensor"), "pair", None),
    )
    return jax.shard_map(
        body, mesh=mesh, in_specs=placed, out_specs=P(("expert", "tensor"), "pair"), check_vma=False
    )
```

time: 242 us -> 77.4 us (0.32)
  waiting for transfers between devices: 120 us -> 0 us
  Pallas kernels: 0 us -> 69 us
  blocking collectives: 67.1 us -> 0 us
  matrix products: 15.8 us -> 0 us
  starting transfers between devices: 14.3 us -> 0 us
  between operations: 13.5 us -> 0.02 us
    reduce_scatter x2 -> x0, waiting for transfers between devices: 89.2 us -> none  [the longest x1 79.8 us: body(): lax.psum_scatter(jnp.dot(context, out_weight, preferred_element_type=jnp....]
    pallas_call x0 -> x1, Pallas kernels: none -> 69 us  [body(): pl.pallas_call(kernel, out_shape=jax.ShapeDtypeStruct((rows, half), BF16)...]
    all_to_all x1 -> x0, blocking collectives: 65.2 us -> none  [body(): lax.all_to_all(outgoing, ('expert', 'tensor'), split_axis=1, concat_axis=...]
    all_to_all x1 -> x0, waiting for transfers between devices: 30.6 us -> none  [body(): lax.all_to_all(summed, ('expert', 'tensor'), split_axis=1, concat_axis=1,...]
    dot_general x5 -> x0, matrix products: 15.8 us -> none  [the longest x1 7.83 us: expert_mlp(): jnp.einsum('ksef,efd->ksed', hidden, w_down, preferred_element_type=jnp.f...]
    all_to_all x1 -> x0, starting transfers between devices: 14.2 us -> none  [body(): lax.all_to_all(summed, ('expert', 'tensor'), split_axis=1, concat_axis=1,...]
    unnamed x15 -> x11, local copies, waits for them, and re-layouts: 1.39 us -> 7.36 us
    reshape x2 -> x1, local copies, waits for them, and re-layouts: 5.49 us -> 0.71 us  [body(): norm_gain.reshape(1, -1)]
  transfers between devices with their start and end apart: 3 -> 0, of which waited for: 3 -> 0; matrix products, arithmetic and copies ran while one was open for 0% -> 0% of each run, Pallas kernels for 0% -> 0%
where the time goes in v1:
time: 77.4 us; the launch traced here: 77.1 us
  Pallas kernels  69 us (89%)
  local copies, waits for them, and re-layouts  8.07 us (10%)
    pallas_call x1, Pallas kernels, body(): pl.pallas_call(kernel, out_shape=jax.ShapeDtypeStruct((rows, half), BF16)...  69 us
    unnamed x11, local copies, waits for them, and re-layouts  7.36 us

profile of v1, /device:TPU:8, one launch (start us, length us, event | category | flops | bytes accessed | tf_op | source)
XLA Modules:
  0.0 77.1 jit_solution(9965009570913268545)
XLA Ops:
  0.0 0.8 copy.10.ids_hbm
  0.8 0.8 copy.11.prob_hbm
  1.5 0.7 reshape.3.gain_hbm
  2.2 0.0 copy-start
  2.2 1.9 %copy-done = bf16[1,4096,384]{2,1,0:T(8,128)(2,1)S(1)} copy-done((bf16[1,4096,384]{2,1,0:T(8,128)(2,1)S(1)}, bf16[1,4096,384]{2,1,0:T(8,128)(2,1)}, u32[]{:S(2)}) %copy-start) | copy-done | bytes 3145752
  4.1 0.0 copy-start.1
  4.1 1.6 %copy-done.1 = bf16[512,2048]{1,0:T(8,128)(2,1)S(1)} copy-done((bf16[512,2048]{1,0:T(8,128)(2,1)S(1)}, bf16[512,2048]{1,0:T(8,128)(2,1)}, u32[]{:S(2)}) %copy-start.1) | copy-done | bytes 2097176
  5.7 0.0 copy-start.2
  5.7 0.9 %copy-done.2 = bf16[128,512]{1,0:T(8,128)(2,1)S(1)} copy-done((bf16[128,512]{1,0:T(8,128)(2,1)S(1)}, bf16[128,512]{1,0:T(8,128)(2,1)}, u32[]{:S(2)}) %copy-start.2) | copy-done | bytes 131096
  6.6 0.0 copy-start.3
  6.6 0.8 %copy-done.3 = bf16[16,2048]{1,0:T(8,128)(2,1)S(1)} copy-done((bf16[16,2048]{1,0:T(8,128)(2,1)S(1)}, bf16[16,2048]{1,0:T(8,128)(2,1)}, u32[]{:S(2)}) %copy-start.3) | copy-done | bytes 65560
  7.5 69.0 %block.1 = bf16[16,2048]{1,0:T(8,128)(2,1)S(1)} custom-call(bf16[128,512]{1,0:T(8,128)(2,1)S(1)} %copy-done.2, bf16[512,2048]{1,0:T(8,128)(2,1)S(1)} %copy-done.1, bf16[16,2048]{1,0:T(8,128)(2,1)S(1)} %copy-done.3, bf16[1,4096]{1,0:T(2,128)(2,1)S(1)} %reshape.3.gain_hbm, s32[16,8]{1,0:T(8,128)S(1)} %copy.10.ids_hbm, f32[16,8]{1,0:T(8,128)S(1)} %copy.11.prob_hbm, ...), custom_call_target="tpu_custom_call" | custom-call | tf_op jit(solution)/shard_map/block/pallas_call | solution.py:338
  76.5 0.6 copy.13
Async XLA Ops:
  2.2 1.9 %copy-start = (bf16[1,4096,384]{2,1,0:T(8,128)(2,1)S(1)}, bf16[1,4096,384]{2,1,0:T(8,128)(2,1)}, u32[]{:S(2)}) copy-start(bf16[1,4096,384]{2,1,0:T(8,128)(2,1)} %wg_hbm.1) | copy-start | bytes 9437188
  4.1 1.6 %copy-start.1 = (bf16[512,2048]{1,0:T(8,128)(2,1)S(1)}, bf16[512,2048]{1,0:T(8,128)(2,1)}, u32[]{:S(2)}) copy-start(bf16[512,2048]{1,0:T(8,128)(2,1)} %ow_hbm.1) | copy-start | bytes 6291460
  5.7 0.9 %copy-start.2 = (bf16[128,512]{1,0:T(8,128)(2,1)S(1)}, bf16[128,512]{1,0:T(8,128)(2,1)}, u32[]{:S(2)}) copy-start(bf16[128,512]{1,0:T(8,128)(2,1)} %ctx_hbm.1) | copy-start | bytes 393220
  6.6 0.8 %copy-start.3 = (bf16[16,2048]{1,0:T(8,128)(2,1)S(1)}, bf16[16,2048]{1,0:T(8,128)(2,1)}, u32[]{:S(2)}) copy-start(bf16[16,2048]{1,0:T(8,128)(2,1)} %res_hbm.1) | copy-start | bytes 196612

commit v2 on v1

v2 whole, which is shorter than its diff:
```python
import functools

import jax
import jax.numpy as jnp
from jax import lax
from jax.experimental import pallas as pl
from jax.experimental.pallas import tpu as pltpu
from jax.sharding import PartitionSpec as P

EPS = 1e-06
MESH = pl.DeviceIdType.MESH
BF16 = jnp.bfloat16
F32 = jnp.float32
ROWS = 16
NZ = 8
NT = 8
NQ = 16
WIDTHS = (512, 512, 512, 512)
CHUNKS = len(WIDTHS)
STARTS = tuple(sum(WIDTHS[:c]) for c in range(CHUNKS))
AHEAD = 3
WAY_OUT = ("T0", "G0", "S3", "G1", "D0", "G2", "U0", "D1", "G3", "F0", "D2", "F1", "M0", "D3", "F2", "M1", "F3", "M2", "M3")
WAY_BACK = ("P0", "P1", "P2", "X0", "P3", "X1", "X2", "E0", "X3", "E1", "E2", "E3")
EXTRA = 128


def dot(a, b):
    return jnp.dot(a, b, preferred_element_type=F32)


def dot_nt(a, b):
    return lax.dot_general(a, b, (((1,), (1,)), ((), ())), preferred_element_type=F32)


def rows16(index):
    return pl.ds(pl.multiple_of(index * ROWS, ROWS), ROWS)


def kernel(
    ctx_hbm, ow_hbm, res_hbm, gain_hbm, ids_hbm, prob_hbm, wg_hbm, wu_hbm, wd_hbm, out_ref,
    ctx, ow, res, gain, ids, prob, wgu, wd,
    attb, ars, stream, meta, metal, table, chi, clo,
    line, disp, xs, acc, hid, outb, ret, mixb, zr,
    ld, ow_sem, w_sem,
    a_send, a_recv, m_sem, wd_sem, g_send, g_recv, d_send, d_recv, f_send, f_recv,
    h_sem, r_send, r_recv, z_send, z_recv,
):
    e, t, p = lax.axis_index("expert"), lax.axis_index("tensor"), lax.axis_index("pair")
    z, x_lo = lax.rem(e, NZ), lax.div(e, NZ)
    y, x_hi = lax.div(t, 2), lax.rem(t, 2)
    x = x_hi * 2 + x_lo
    q = x_lo * NT + t
    half = ow.shape[1]
    ff = wg_hbm.shape[2]
    slots = NQ * ROWS
    tokens = NZ * ROWS
    partner = (e, t, 1 - p)

    def along(j):
        return lax.rem(z + j, NZ)

    def z_peer(j):
        return (x_lo * NZ + along(j), t, p)

    def plane_peer(j):
        px, py = lax.rem(x + lax.rem(j, 4), 4), lax.rem(y + lax.div(j, 4), 4)
        plo, pt = lax.rem(px, 2), py * 2 + lax.div(px, 2)
        return plo * NT + pt, (plo * NZ + z, pt, p)

    def each(count, fn):
        def step(j, carry):
            fn(j)
            return carry
        lax.fori_loop(1, count, step, 0)

    def remote(src, dst, send, recv, device):
        return pltpu.make_async_remote_copy(
            src_ref=src, dst_ref=dst, send_sem=send, recv_sem=recv,
            device_id=device, device_id_type=MESH,
        )

    def wait_bytes(ref, sem):
        pltpu.make_async_copy(ref, ref, sem).wait()

    def cols(c):
        return pl.ds(STARTS[c], WIDTHS[c])

    def more(c):
        return pl.ds(STARTS[c], WIDTHS[c] + (EXTRA if c == CHUNKS - 1 else 0))

    def mine(index):
        return pl.ds(pl.multiple_of(index * half, half), half)

    pending = []

    loads = [
        pltpu.make_async_copy(ctx_hbm, ctx, ld.at[0]),
        pltpu.make_async_copy(res_hbm, res, ld.at[1]),
        pltpu.make_async_copy(gain_hbm.at[mine(p)], gain, ld.at[2]),
        pltpu.make_async_copy(ids_hbm, ids, ld.at[3]),
        pltpu.make_async_copy(prob_hbm, prob, ld.at[4]),
    ]
    ow_loads = [
        pltpu.make_async_copy(ow_hbm.at[:, cols(c)], ow.at[:, cols(c)], ow_sem.at[c])
        for c in range(CHUNKS)
    ]
    w_loads = []
    for k, side in enumerate((p, 1 - p)):
        w_loads.append(pltpu.make_async_copy(
            wg_hbm.at[0, mine(side), :], wgu.at[k, :, pl.ds(0, ff)], w_sem.at[2 * k]))
        w_loads.append(pltpu.make_async_copy(
            wu_hbm.at[0, mine(side), :], wgu.at[k, :, pl.ds(ff, ff)], w_sem.at[2 * k + 1]))
    wd_load = pltpu.make_async_copy(wd_hbm.at[0, :, mine(p)], wd.at[0], w_sem.at[4])
    for copy in loads[:1] + ow_loads + loads[1:]:
        copy.start()

    barrier = pltpu.get_barrier_semaphore()
    each(NQ, lambda j: pl.semaphore_signal(barrier, inc=1, device_id=plane_peer(j)[1], device_id_type=MESH))
    each(NZ, lambda j: pl.semaphore_signal(barrier, inc=1, device_id=z_peer(j), device_id_type=MESH))
    pl.semaphore_signal(barrier, inc=1, device_id=partner, device_id_type=MESH)

    def project(c):
        ow_loads[c].wait()
        attb[:, cols(c)] = dot(ctx[...], ow[:, cols(c)]).astype(BF16)

    def scatter_heads(c):
        def send(j):
            pt = lax.rem(t + j, NT)
            remote(attb.at[rows16(pt), cols(c)], ars.at[rows16(t), cols(c)],
                   a_send.at[c], a_recv.at[c], (e, pt, p)).start()
        each(NT, send)
        pending.append(lambda: wait_bytes(ars.at[pl.ds(0, (NT - 1) * ROWS), cols(c)], a_send.at[c]))

    loads[0].wait()
    project(0)
    pl.semaphore_wait(barrier, NZ - 1 + NQ - 1 + 1)
    scatter_heads(0)
    for c in range(1, AHEAD):
        project(c)
        scatter_heads(c)
    for copy in w_loads + [wd_load]:
        copy.start()

    for copy in loads[1:]:
        copy.wait()
    weights = prob[...] / jnp.sum(prob[...], axis=0, keepdims=True)
    named = ids[...]
    experts = lax.broadcasted_iota(jnp.int32, (128, ROWS), 0)
    mark = jnp.zeros((128, ROWS), F32)
    spread = jnp.zeros((128, ROWS), F32)
    for k in range(named.shape[0]):
        same = experts == named[k:k + 1, :]
        mark = jnp.where(same, 1.0, mark)
        spread = jnp.where(same, weights[k:k + 1, :], spread)
    before = lax.broadcasted_iota(jnp.int32, (ROWS, ROWS), 1)
    after = lax.broadcasted_iota(jnp.int32, (ROWS, ROWS), 0)
    earlier = (before < after).astype(F32).astype(BF16)
    same_row = (before == after).astype(F32).astype(BF16)
    mark = mark.astype(BF16)
    high = spread.astype(BF16)
    low = (spread - high.astype(F32)).astype(BF16)
    meta[0] = (dot_nt(same_row, mark) * (1.0 + dot_nt(earlier, mark))).astype(BF16)
    meta[1] = dot_nt(same_row, high).astype(BF16)
    meta[2] = dot_nt(same_row, low).astype(BF16)
    metal[:, rows16(z), :] = meta[...]
    each(NZ, lambda j: remote(meta, metal.at[:, rows16(z), :], m_sem.at[0], m_sem.at[1], z_peer(j)).start())
    pending.append(lambda: wait_bytes(metal.at[:, pl.ds(0, (NZ - 1) * ROWS), :], m_sem.at[0]))
    wd_swap = remote(wd_hbm.at[0, :, mine(1 - p)], wd.at[1], wd_sem.at[0], wd_sem.at[1], partner)
    wd_swap.start()
    pending.append(wd_swap.wait_send)

    def expert_of(row):
        place = lax.shift_right_logical(row, 4)
        return (lax.shift_right_logical(place, 3) * (NZ * NT) + z * NT + (place & (NT - 1)))

    def fits(row, token, codes):
        wanted = ((row & 1) + 1).astype(F32)
        same = (lax.shift_right_logical(row, 1) & (NZ - 1)) == lax.shift_right_logical(token, 4)
        return same & (codes == wanted)

    def iota(rows, columns, axis):
        return lax.broadcasted_iota(jnp.int32, (rows, columns), axis)

    def picker():
        return (iota(slots, 128, 1) == expert_of(iota(slots, 128, 0))).astype(F32).astype(BF16)

    def down_table():
        wait_bytes(metal.at[:, pl.ds(0, (NZ - 1) * ROWS), :], m_sem.at[1])
        codes = dot_nt(picker(), metal[0])
        chosen = fits(iota(slots, tokens, 0), iota(slots, tokens, 1), codes)
        table[...] = jnp.where(chosen, 1.0, 0.0).astype(BF16)

    def up_tables():
        pick = picker()
        chosen = fits(iota(tokens, slots, 1), iota(tokens, slots, 0), dot_nt(metal[0], pick))
        chi[...] = jnp.where(chosen, dot_nt(metal[1], pick), 0.0).astype(BF16)
        clo[...] = jnp.where(chosen, dot_nt(metal[2], pick), 0.0).astype(BF16)

    squares = [jnp.zeros((ROWS, 1), F32)]

    def gather_heads(c):
        ars[rows16(t), cols(c)] = attb[rows16(t), cols(c)]
        wait_bytes(ars.at[pl.ds(0, (NT - 1) * ROWS), cols(c)], a_recv.at[c])
        total = res[:, cols(c)].astype(F32)
        heads = ars[0:ROWS, cols(c)].astype(F32)
        for k in range(1, NT):
            heads += ars[k * ROWS:(k + 1) * ROWS, cols(c)].astype(F32)
        part = (total + heads).astype(BF16)
        stream[:, cols(c)] = part
        wide = part.astype(F32)
        squares[0] = squares[0] + jnp.sum(wide * wide, axis=1, keepdims=True)
        line[rows16(z), cols(c)] = (wide * gain[cols(c)].astype(F32)[None, :]).astype(BF16)
        if c == CHUNKS - 1:
            top = squares[0].astype(BF16).astype(F32)
            middle = (squares[0] - top).astype(BF16).astype(F32)
            lane = iota(ROWS, EXTRA, 1)
            parts = jnp.where(lane == 0, top, jnp.where(lane == 1, middle, squares[0] - top - middle))
            line[rows16(z), pl.ds(half, EXTRA)] = jnp.where(lane < 3, parts, 0.0).astype(BF16)
        each(NZ, lambda j: remote(line.at[rows16(z), more(c)], line.at[rows16(z), more(c)],
                                  g_send.at[c], g_recv.at[c], z_peer(j)).start())
        pending.append(lambda: wait_bytes(line.at[pl.ds(0, tokens - ROWS), more(c)], g_send.at[c]))

    def dispatch(c):
        wait_bytes(line.at[pl.ds(0, tokens - ROWS), more(c)], g_recv.at[c])
        disp[:, more(c)] = dot(table[...], line[:, more(c)]).astype(BF16)

        def send(j):
            pq, device = plane_peer(j)
            remote(disp.at[rows16(pq), more(c)], xs.at[0, rows16(q), more(c)],
                   d_send.at[c], d_recv.at[c], device).start()
        each(NQ, send)
        pending.append(lambda: wait_bytes(xs.at[0, pl.ds(0, slots - ROWS), more(c)], d_send.at[c]))
        xs[0, rows16(q), more(c)] = disp[rows16(q), more(c)]

    forwards = [
        remote(xs.at[0, :, more(c)], xs.at[1, :, more(c)], f_send.at[c], f_recv.at[c], partner)
        for c in range(CHUNKS)
    ]

    def forward(c):
        wait_bytes(xs.at[0, pl.ds(0, slots - ROWS), more(c)], d_recv.at[c])
        forwards[c].start()
        pending.append(forwards[c].wait_send)

    def multiply(c):
        own = dot(xs[0, :, cols(c)], wgu[0, cols(c), :])
        forwards[c].wait_recv()
        both = own + dot(xs[1, :, cols(c)], wgu[1, cols(c), :])
        if c == 0:
            acc[...] = both
        else:
            acc[...] += both

    def head_start(c):
        project(c)
        scatter_heads(c)

    def tables():
        up_tables()
        for copy in w_loads:
            copy.wait()

    steps = {
        "S": head_start, "G": gather_heads, "D": dispatch, "F": forward, "M": multiply,
        "T": lambda c: down_table(), "U": lambda c: tables(),
    }
    for name in WAY_OUT:
        steps[name[0]](int(name[1]))

    sums = jnp.sum(xs[0, :, pl.ds(half, EXTRA)].astype(F32) + xs[1, :, pl.ds(half, EXTRA)].astype(F32),
                   axis=1, keepdims=True)
    scale = lax.rsqrt(sums * (1.0 / (2 * half)) + EPS)
    gate, up = acc[:, 0:ff] * scale, acc[:, ff:2 * ff] * scale
    hid[0] = (gate / (1.0 + jnp.exp(-gate)) * up).astype(BF16)
    hid_swap = remote(hid.at[0], hid.at[1], h_sem.at[0], h_sem.at[1], partner)
    hid_swap.start()
    pending.append(hid_swap.wait_send)
    wd_load.wait()
    wd_swap.wait_recv()
    hid_swap.wait_recv()

    def produce(c):
        outb[:, cols(c)] = (dot(hid[0], wd[0, :, cols(c)]) + dot(hid[1], wd[1, :, cols(c)])).astype(BF16)

        def send(j):
            pq, device = plane_peer(j)
            remote(outb.at[rows16(pq), cols(c)], ret.at[rows16(q), cols(c)],
                   r_send.at[c], r_recv.at[c], device).start()
        each(NQ, send)
        pending.append(lambda: wait_bytes(ret.at[pl.ds(0, slots - ROWS), cols(c)], r_send.at[c]))
        ret[rows16(q), cols(c)] = outb[rows16(q), cols(c)]

    def mix(c):
        wait_bytes(ret.at[pl.ds(0, slots - ROWS), cols(c)], r_recv.at[c])
        mixb[:, cols(c)] = (dot(chi[...], ret[:, cols(c)]) + dot(clo[...], ret[:, cols(c)])).astype(BF16)

        def send(j):
            remote(mixb.at[rows16(along(j)), cols(c)], zr.at[rows16(z), cols(c)],
                   z_send.at[c], z_recv.at[c], z_peer(j)).start()
        each(NZ, send)
        pending.append(lambda: wait_bytes(zr.at[pl.ds(0, tokens - ROWS), cols(c)], z_send.at[c]))
        zr[rows16(z), cols(c)] = mixb[rows16(z), cols(c)]

    def finish(c):
        wait_bytes(zr.at[pl.ds(0, tokens - ROWS), cols(c)], z_recv.at[c])
        total = stream[:, cols(c)].astype(F32)
        for k in range(NZ):
            total += zr[k * ROWS:(k + 1) * ROWS, cols(c)].astype(F32)
        out_ref[:, cols(c)] = total.astype(BF16)

    steps = {"P": produce, "X": mix, "E": finish}
    for name in WAY_BACK:
        steps[name[0]](int(name[1]))

    for wait in pending:
        wait()


def body(context, out_weight, residual, norm_gain, expert_ids, route_prob, w_gate, w_up, w_down):
    rows, half = residual.shape
    group, depth = context.shape
    ff = w_gate.shape[2]
    slots, tokens = NQ * ROWS, NZ * ROWS
    dma = pltpu.SemaphoreType.DMA
    scratch = [
        pltpu.VMEM((group, depth), BF16),
        pltpu.VMEM((depth, half), BF16),
        pltpu.VMEM((rows, half), BF16),
        pltpu.VMEM((half,), BF16),
        pltpu.VMEM(expert_ids.shape[::-1], jnp.int32),
        pltpu.VMEM(route_prob.shape[::-1], F32),
        pltpu.VMEM((2, half, 2 * ff), BF16),
        pltpu.VMEM((2, ff, half), BF16),
        pltpu.VMEM((group, half), BF16),
        pltpu.VMEM((group, half), BF16),
        pltpu.VMEM((rows, half), BF16),
        pltpu.VMEM((3, rows, 128), BF16),
        pltpu.VMEM((3, tokens, 128), BF16),
        pltpu.VMEM((slots, tokens), BF16),
        pltpu.VMEM((tokens, slots), BF16),
        pltpu.VMEM((tokens, slots), BF16),
        pltpu.VMEM((tokens, half + EXTRA), BF16),
        pltpu.VMEM((slots, half + EXTRA), BF16),
        pltpu.VMEM((2, slots, half + EXTRA), BF16),
        pltpu.VMEM((slots, 2 * ff), F32),
        pltpu.VMEM((2, slots, ff), BF16),
        pltpu.VMEM((slots, half), BF16),
        pltpu.VMEM((slots, half), BF16),
        pltpu.VMEM((tokens, half), BF16),
        pltpu.VMEM((tokens, half), BF16),
        dma((5,)), dma((CHUNKS,)), dma((5,)),
        dma((CHUNKS,)), dma((CHUNKS,)), dma((2,)), dma((2,)),
        dma((CHUNKS,)), dma((CHUNKS,)), dma((CHUNKS,)), dma((CHUNKS,)),
        dma((CHUNKS,)), dma((CHUNKS,)),
        dma((2,)), dma((CHUNKS,)), dma((CHUNKS,)), dma((CHUNKS,)), dma((CHUNKS,)),
    ]
    return pl.pallas_call(
        kernel,
        out_shape=jax.ShapeDtypeStruct((rows, half), BF16),
        in_specs=[pl.BlockSpec(memory_space=pltpu.HBM)] * 9,
        out_specs=pl.BlockSpec(memory_space=pltpu.VMEM),
        scratch_shapes=scratch,
        compiler_params=pltpu.CompilerParams(
            collective_id=0, has_side_effects=True, vmem_limit_bytes=60 * 1024 * 1024
        ),
        name="block",
    )(
        context, out_weight, residual, norm_gain, expert_ids.T, route_prob.T,
        w_gate, w_up, w_down,
    )


def solution(mesh):
    placed = (
        P("expert", "tensor"),
        P("tensor", "pair"),
        P(("expert", "tensor"), "pair"),
        P(),
        P(("expert", "tensor"), None),
        P(("expert", "tensor"), None),
        P(("expert", "tensor"), None, "pair"),
        P(("expert", "tensor"), None, "pair"),
        P(("expert", "tensor"), "pair", None),
    )
    return jax.shard_map(
        body, mesh=mesh, in_specs=placed, out_specs=P(("expert", "tensor"), "pair"), check_vma=False
    )
```

time: 77.4 us -> 67.4 us (0.87)
  local copies, waits for them, and re-layouts: 8.07 us -> 1.47 us
  Pallas kernels: 69 us -> 65.6 us
    unnamed x11 -> x1, local copies, waits for them, and re-layouts: 7.36 us -> 1.47 us
    pallas_call x1, Pallas kernels: 69 us -> 65.6 us  [body(): pl.pallas_call(kernel, out_shape=jax.ShapeDtypeStruct((rows, half), BF16)...]
where the time goes in v2:
time: 67.4 us; the launch traced here: 67 us
  Pallas kernels  65.6 us (97%)
  local copies, waits for them, and re-layouts  1.47 us (2%)
    pallas_call x1, Pallas kernels, body(): pl.pallas_call(kernel, out_shape=jax.ShapeDtypeStruct((rows, half), BF16)...  65.6 us
    unnamed x1, local copies, waits for them, and re-layouts  1.47 us

profile of v2, /device:TPU:8, one launch (start us, length us, event | category | flops | bytes accessed | tf_op | source)
XLA Modules:
  0.0 67.0 jit_solution(11166721768999106595)
XLA Ops:
  0.0 65.6 %block.1 = bf16[16,2048]{1,0:T(8,128)(2,1)} custom-call(bf16[128,512]{1,0:T(8,128)(2,1)} %ctx_hbm.1, bf16[512,2048]{1,0:T(8,128)(2,1)} %ow_hbm.1, bf16[16,2048]{1,0:T(8,128)(2,1)} %res_hbm.1, bf16[4096]{0:T(1024)(128)(2,1)} %gain_hbm.1, s32[8,16]{1,0:T(8,128)} %bitcast.2, f32[8,16]{1,0:T(8,128)} %bitcast.3, bf16[1,4096,384]{2,1,0:T(8,128)(2,1)} %wg_hbm.1, ...), custom_call_target="tpu_custom_call" | custom-call | tf_op jit(solution)/shard_map/block/pallas_call | solution.py:357
  65.6 1.5 %copy.11 = bf16[16,2048]{1,0:T(8,128)(2,1)} copy(bf16[16,2048]{1,0:T(8,128)(2,1)} %block.1) | data formatting | bytes 131072

commit v3 on v2

--- a/solution.py
+++ b/solution.py
@@ -18,9 +18,9 @@
 WIDTHS = (512, 512, 512, 512)
 CHUNKS = len(WIDTHS)
 STARTS = tuple(sum(WIDTHS[:c]) for c in range(CHUNKS))
-AHEAD = 3
-WAY_OUT = ("T0", "G0", "S3", "G1", "D0", "G2", "U0", "D1", "G3", "F0", "D2", "F1", "M0", "D3", "F2", "M1", "F3", "M2", "M3")
-WAY_BACK = ("P0", "P1", "P2", "X0", "P3", "X1", "X2", "E0", "X3", "E1", "E2", "E3")
+AHEAD = 2
+WAY_OUT = ("T0", "G0", "S2", "G1", "S3", "D0", "G2", "D1", "G3", "F0", "D2", "U0", "F1", "D3", "M0", "F2", "M1", "F3", "M2", "M3")
+WAY_BACK = ("P0", "P1", "P2", "X0", "P3", "Q0", "X1", "X2", "E0", "X3", "E1", "E2", "E3")
 EXTRA = 128
 
 
@@ -43,7 +43,7 @@
     line, disp, xs, acc, hid, outb, ret, mixb, zr,
     ld, ow_sem, w_sem,
     a_send, a_recv, m_sem, wd_sem, g_send, g_recv, d_send, d_recv, f_send, f_recv,
-    h_sem, r_send, r_recv, z_send, z_recv,
+    h_sem, r_send, r_recv, z_send, z_recv, o_sem, result,
 ):
     e, t, p = lax.axis_index("expert"), lax.axis_index("tensor"), lax.axis_index("pair")
     z, x_lo = lax.rem(e, NZ), lax.div(e, NZ)
@@ -92,6 +92,10 @@
         return pl.ds(pl.multiple_of(index * half, half), half)
 
     pending = []
+
+    def drain(count):
+        for _ in range(count):
+            pending.pop(0)()
 
     loads = [
         pltpu.make_async_copy(ctx_hbm, ctx, ld.at[0]),
@@ -110,7 +114,7 @@
             wg_hbm.at[0, mine(side), :], wgu.at[k, :, pl.ds(0, ff)], w_sem.at[2 * k]))
         w_loads.append(pltpu.make_async_copy(
             wu_hbm.at[0, mine(side), :], wgu.at[k, :, pl.ds(ff, ff)], w_sem.at[2 * k + 1]))
-    wd_load = pltpu.make_async_copy(wd_hbm.at[0, :, mine(p)], wd.at[0], w_sem.at[4])
+    wd_load = pltpu.make_async_copy(wd_hbm.at[0, :, mine(p)], wd.at[pl.ds(0, ff), :], w_sem.at[4])
     for copy in loads[:1] + ow_loads + loads[1:]:
         copy.start()
 
@@ -165,7 +169,7 @@
     metal[:, rows16(z), :] = meta[...]
     each(NZ, lambda j: remote(meta, metal.at[:, rows16(z), :], m_sem.at[0], m_sem.at[1], z_peer(j)).start())
     pending.append(lambda: wait_bytes(metal.at[:, pl.ds(0, (NZ - 1) * ROWS), :], m_sem.at[0]))
-    wd_swap = remote(wd_hbm.at[0, :, mine(1 - p)], wd.at[1], wd_sem.at[0], wd_sem.at[1], partner)
+    wd_swap = remote(wd_hbm.at[0, :, mine(1 - p)], wd.at[pl.ds(ff, ff), :], wd_sem.at[0], wd_sem.at[1], partner)
     wd_swap.start()
     pending.append(wd_swap.wait_send)
 
@@ -271,16 +275,17 @@
                    axis=1, keepdims=True)
     scale = lax.rsqrt(sums * (1.0 / (2 * half)) + EPS)
     gate, up = acc[:, 0:ff] * scale, acc[:, ff:2 * ff] * scale
-    hid[0] = (gate / (1.0 + jnp.exp(-gate)) * up).astype(BF16)
-    hid_swap = remote(hid.at[0], hid.at[1], h_sem.at[0], h_sem.at[1], partner)
+    hid[:, 0:ff] = (gate / (1.0 + jnp.exp(-gate)) * up).astype(BF16)
+    hid_swap = remote(hid.at[:, pl.ds(0, ff)], hid.at[:, pl.ds(ff, ff)], h_sem.at[0], h_sem.at[1], partner)
     hid_swap.start()
     pending.append(hid_swap.wait_send)
     wd_load.wait()
     wd_swap.wait_recv()
     hid_swap.wait_recv()
+    early = len(pending)
 
     def produce(c):
-        outb[:, cols(c)] = (dot(hid[0], wd[0, :, cols(c)]) + dot(hid[1], wd[1, :, cols(c)])).astype(BF16)
+        outb[:, cols(c)] = dot(hid[...], wd[:, cols(c)]).astype(BF16)
 
         def send(j):
             pq, device = plane_peer(j)
@@ -306,14 +311,16 @@
         total = stream[:, cols(c)].astype(F32)
         for k in range(NZ):
             total += zr[k * ROWS:(k + 1) * ROWS, cols(c)].astype(F32)
-        out_ref[:, cols(c)] = total.astype(BF16)
-
-    steps = {"P": produce, "X": mix, "E": finish}
+        result[:, cols(c)] = total.astype(BF16)
+        leave = pltpu.make_async_copy(result.at[:, cols(c)], out_ref.at[:, cols(c)], o_sem.at[c])
+        leave.start()
+        pending.append(leave.wait)
+
+    steps = {"P": produce, "X": mix, "E": finish, "Q": lambda c: drain(early if c == 0 else CHUNKS)}
     for name in WAY_BACK:
         steps[name[0]](int(name[1]))
 
-    for wait in pending:
-        wait()
+    drain(len(pending))
 
 
 def body(context, out_weight, residual, norm_gain, expert_ids, route_prob, w_gate, w_up, w_down):
@@ -330,7 +337,7 @@
         pltpu.VMEM(expert_ids.shape[::-1], jnp.int32),
         pltpu.VMEM(route_prob.shape[::-1], F32),
         pltpu.VMEM((2, half, 2 * ff), BF16),
-        pltpu.VMEM((2, ff, half), BF16),
+        pltpu.VMEM((2 * ff, half), BF16),
         pltpu.VMEM((group, half), BF16),
         pltpu.VMEM((group, half), BF16),
         pltpu.VMEM((rows, half), BF16),
@@ -343,7 +350,7 @@
         pltpu.VMEM((slots, half + EXTRA), BF16),
         pltpu.VMEM((2, slots, half + EXTRA), BF16),
         pltpu.VMEM((slots, 2 * ff), F32),
-        pltpu.VMEM((2, slots, ff), BF16),
+        pltpu.VMEM((slots, 2 * ff), BF16),
         pltpu.VMEM((slots, half), BF16),
         pltpu.VMEM((slots, half), BF16),
         pltpu.VMEM((tokens, half), BF16),
@@ -352,13 +359,14 @@
         dma((CHUNKS,)), dma((CHUNKS,)), dma((2,)), dma((2,)),
         dma((CHUNKS,)), dma((CHUNKS,)), dma((CHUNKS,)), dma((CHUNKS,)),
         dma((CHUNKS,)), dma((CHUNKS,)),
-        dma((2,)), dma((CHUNKS,)), dma((CHUNKS,)), dma((CHUNKS,)), dma((CHUNKS,)),
+        dma((2,)), dma((CHUNKS,)), dma((CHUNKS,)), dma((CHUNKS,)), dma((CHUNKS,)), dma((CHUNKS,)),
+        pltpu.VMEM((rows, half), BF16),
     ]
     return pl.pallas_call(
         kernel,
         out_shape=jax.ShapeDtypeStruct((rows, half), BF16),
         in_specs=[pl.BlockSpec(memory_space=pltpu.HBM)] * 9,
-        out_specs=pl.BlockSpec(memory_space=pltpu.VMEM),
+        out_specs=pl.BlockSpec(memory_space=pltpu.HBM),
         scratch_shapes=scratch,
         compiler_params=pltpu.CompilerParams(
             collective_id=0, has_side_effects=True, vmem_limit_bytes=60 * 1024 * 1024

time: 67.4 us -> 66.2 us (0.982)
  Pallas kernels: 65.6 us -> 64.1 us
    pallas_call x1, Pallas kernels: 65.6 us -> 64.1 us  [body(): pl.pallas_call(kernel, out_shape=jax.ShapeDtypeStruct((rows, half), BF16)...]
where the time goes in v3:
time: 66.2 us; the launch traced here: 65.6 us
  Pallas kernels  64.1 us (97%)
  local copies, waits for them, and re-layouts  1.47 us (2%)
    pallas_call x1, Pallas kernels, body(): pl.pallas_call(kernel, out_shape=jax.ShapeDtypeStruct((rows, half), BF16)...  64.1 us
    unnamed x1, local copies, waits for them, and re-layouts  1.47 us

profile of v3, /device:TPU:8, one launch (start us, length us, event | category | flops | bytes accessed | tf_op | source)
XLA Modules:
  0.0 65.6 jit_solution(16812728997868724916)
XLA Ops:
  0.0 64.1 %block.1 = bf16[16,2048]{1,0:T(8,128)(2,1)} custom-call(bf16[128,512]{1,0:T(8,128)(2,1)} %ctx_hbm.1, bf16[512,2048]{1,0:T(8,128)(2,1)} %ow_hbm.1, bf16[16,2048]{1,0:T(8,128)(2,1)} %res_hbm.1, bf16[4096]{0:T(1024)(128)(2,1)} %gain_hbm.1, s32[8,16]{1,0:T(8,128)} %bitcast.2, f32[8,16]{1,0:T(8,128)} %bitcast.3, bf16[1,4096,384]{2,1,0:T(8,128)(2,1)} %wg_hbm.1, ...), custom_call_target="tpu_custom_call" | custom-call | tf_op jit(solution)/shard_map/block/pallas_call | solution.py:365
  64.1 1.5 %copy.11 = bf16[16,2048]{1,0:T(8,128)(2,1)} copy(bf16[16,2048]{1,0:T(8,128)(2,1)} %block.1) | data formatting | bytes 131072

commit v4 on v3

--- a/solution.py
+++ b/solution.py
@@ -221,7 +221,7 @@
             parts = jnp.where(lane == 0, top, jnp.where(lane == 1, middle, squares[0] - top - middle))
             line[rows16(z), pl.ds(half, EXTRA)] = jnp.where(lane < 3, parts, 0.0).astype(BF16)
         each(NZ, lambda j: remote(line.at[rows16(z), more(c)], line.at[rows16(z), more(c)],
-                                  g_send.at[c], g_recv.at[c], z_peer(j)).start())
+                                  g_send.at[c], g_recv.at[c], z_peer(lax.rem(j * 3, NZ))).start())
         pending.append(lambda: wait_bytes(line.at[pl.ds(0, tokens - ROWS), more(c)], g_send.at[c]))
 
     def dispatch(c):
@@ -300,6 +300,7 @@
         mixb[:, cols(c)] = (dot(chi[...], ret[:, cols(c)]) + dot(clo[...], ret[:, cols(c)])).astype(BF16)
 
         def send(j):
+            j = lax.rem(j * 3, NZ)
             remote(mixb.at[rows16(along(j)), cols(c)], zr.at[rows16(z), cols(c)],
                    z_send.at[c], z_recv.at[c], z_peer(j)).start()
         each(NZ, send)

time: 66.2 us -> 64.3 us (0.971)
  Pallas kernels: 64.1 us -> 62.6 us
    pallas_call x1, Pallas kernels: 64.1 us -> 62.6 us  [body(): pl.pallas_call(kernel, out_shape=jax.ShapeDtypeStruct((rows, half), BF16)...]
where the time goes in v4:
time: 64.3 us; the launch traced here: 64.1 us
  Pallas kernels  62.6 us (97%)
  local copies, waits for them, and re-layouts  1.47 us (2%)
    pallas_call x1, Pallas kernels, body(): pl.pallas_call(kernel, out_shape=jax.ShapeDtypeStruct((rows, half), BF16)...  62.6 us
    unnamed x1, local copies, waits for them, and re-layouts  1.47 us

profile of v4, /device:TPU:8, one launch (start us, length us, event | category | flops | bytes accessed | tf_op | source)
XLA Modules:
  0.0 64.1 jit_solution(10938704169888323874)
XLA Ops:
  0.0 62.6 %block.1 = bf16[16,2048]{1,0:T(8,128)(2,1)} custom-call(bf16[128,512]{1,0:T(8,128)(2,1)} %ctx_hbm.1, bf16[512,2048]{1,0:T(8,128)(2,1)} %ow_hbm.1, bf16[16,2048]{1,0:T(8,128)(2,1)} %res_hbm.1, bf16[4096]{0:T(1024)(128)(2,1)} %gain_hbm.1, s32[8,16]{1,0:T(8,128)} %bitcast.2, f32[8,16]{1,0:T(8,128)} %bitcast.3, bf16[1,4096,384]{2,1,0:T(8,128)(2,1)} %wg_hbm.1, ...), custom_call_target="tpu_custom_call" | custom-call | tf_op jit(solution)/shard_map/block/pallas_call | solution.py:366
  62.6 1.5 %copy.11 = bf16[16,2048]{1,0:T(8,128)(2,1)} copy(bf16[16,2048]{1,0:T(8,128)(2,1)} %block.1) | data formatting | bytes 131072
